TPU v7x, 32 devices: a whole 2x2x4 slice. The times are simulated.
32 devices in a mesh: gz: 4 (over y, x), xy: 8 (over z, core).
Axes of the slice: x: 2, y: 2, z: 4, core: 2. Of those that a mesh axis runs over, the one named last changes fastest.
Arguments:
- residual_in: float32 [144, 32, 8, 128], P(None, 'gz', 'xy'), may hold values from -75 to 75
- ritz_vector: float32 [144, 32, 8, 128], P(None, 'gz', 'xy'), may hold values from -14.4 to 14.4
- density: float32 [32, 8, 128], P('gz', 'xy'), may hold values from 0 to 1
- pml_flags: int32 [32, 8, 128], P('gz', 'xy'), may hold values 0 or 1
- design_mask: int32 [32, 8, 128], P('gz', 'xy'), may hold values 0 or 1
- k_base: float32 [144, 144], replicated, may hold values from -0.5 to 4.5
- k_rho: float32 [144, 144], replicated, may hold values from -0.5 to 0.5
- k_pml: float32 [144, 144], replicated, may hold values from -0.5 to 0.5
- k_face: float32 [6, 144, 144], replicated, may hold values from -0.5 to 0.5
- shift_re: float32 [], replicated, may hold values from 0.5 to 2
- shift_im: float32 [], replicated, may hold values from 0.2 to 1
Outputs:
- correction: float32 [144, 32, 8, 128], P(None, 'gz', 'xy')
- filtered: float32 [32, 8, 128], P('gz', 'xy')
All inputs are finite; a program needn't handle non-finite values. No bound on the sum of `pml_flags` or of `design_mask` on one device may be relied on, other than what follows from the above.
Results may differ from a plain program's by a relative error of at most 0.0055.
Values sent between devices are 32-bit elements; how exact they have to be, the bound alone decides.
A program may use at most 64 MiB of HBM per device.

v0:
```python
import functools

import jax
import jax.numpy as jnp
from jax import lax
from jax.experimental import pallas as pl
from jax.experimental.pallas import tpu as pltpu
from jax.sharding import PartitionSpec as P

TX = 4
EY = 8
EX = 16
LANES = EY * EX
REACH = 5
MESH = pl.DeviceIdType.MESH
F32 = jnp.float32
BF16 = jnp.bfloat16


def split(x):
    hi = x.astype(BF16)
    return hi, (x - hi.astype(F32)).astype(BF16)


def fold(x):
    return jnp.sum(x.reshape(x.shape[0] // 8, 8, LANES), axis=0)


def pair_terms(u, f):
    half = u.shape[0] // 2
    ur, ui, fr, fi = u[:half], u[half:], f[:half], f[half:]
    return fold(ur * fr + ui * fi), fold(ur * fi - ui * fr)


def removed_part(u, re, im):
    half = u.shape[0] // 2
    ur, ui = u[:half], u[half:]
    return jnp.concatenate([re * ur - im * ui, re * ui + im * ur], axis=0)


def mm(a, b):
    return jnp.dot(a, b, preferred_element_type=F32)


def kernel(
    G, X, B, depth,
    res, rit, den, pml, msk, kb, kr, kp, kf, sre, sim,
    cor, fil,
    kface, kself, hsend, hrecv, V, H, I1, st, st2, p1, p2,
    sens, zrecv, zpad, lat, lrecv, wlat,
    s1s, s1r, s2s, s2r, hss, hrs, zss, zrs, lss, lrs,
):
    g = lax.axis_index("gz")
    t = lax.axis_index("xy")
    col = lax.rem(t, TX)
    row = t // TX
    TY = X // TX
    count = float(B * depth * LANES * G * X)

    def gz_peer(o):
        return {"gz": lax.rem(g + o + G, G)}

    def xy_peer(o):
        return {"xy": lax.rem(t + o + X, X)}

    barrier = pltpu.get_barrier_semaphore()
    for o in range(1, G):
        pl.semaphore_signal(barrier, inc=1, device_id=gz_peer(o), device_id_type=MESH)
    for o in range(1, X):
        pl.semaphore_signal(barrier, inc=1, device_id=xy_peer(o), device_id_type=MESH)

    def rlayer(ref, z):
        return ref[pl.ds(z, B, stride=depth), :]

    def remote(src, dst, ss, rs, dev):
        return pltpu.make_async_remote_copy(
            src_ref=src, dst_ref=dst, send_sem=ss, recv_sem=rs,
            device_id=dev, device_id_type=MESH,
        )

    def stage1(r):
        return [
            remote(st.at[r], p1.at[r, o - 1], s1s.at[r, o - 1], s1r.at[r, o - 1], gz_peer(o))
            for o in range(1, G)
        ]

    def stage2(r):
        return [
            remote(st2.at[r], p2.at[r, o - 1], s2s.at[r, o - 1], s2r.at[r, o - 1], xy_peer(o))
            for o in range(1, X)
        ]

    def sum_start(r, a, b, c):
        rows = [jnp.sum(v, axis=0, keepdims=True) for v in (a, b, c)]
        st[r] = jnp.concatenate(rows + [jnp.zeros((5, LANES), F32)], axis=0)
        for copy in stage1(r):
            copy.start()

    def sum_middle(r):
        for copy in stage1(r):
            copy.wait()
        total = st[r]
        for o in range(G - 1):
            total = total + p1[r, o]
        st2[r] = total
        for copy in stage2(r):
            copy.start()

    def sum_end(r):
        for copy in stage2(r):
            copy.wait()
        total = st2[r]
        for o in range(X - 1):
            total = total + p2[r, o]
        total = jnp.sum(total, axis=1, keepdims=True)
        return total[0:1], total[1:2], total[2:3]

    faces = [
        (gz_peer(-1), g > 0, g < G - 1),
        (gz_peer(1), g < G - 1, g > 0),
        (xy_peer(-TX), row > 0, row < TY - 1),
        (xy_peer(TX), row < TY - 1, row > 0),
        (xy_peer(-1), col > 0, col < TX - 1),
        (xy_peer(1), col < TX - 1, col > 0),
    ]

    def halo(s, k):
        src = hsend.at[s, k]
        if s == 2 and k < 2:
            src = I1.at[0 if k == 0 else depth - 1]
        return remote(src, hrecv.at[s, k], hss.at[s, k], hrs.at[s, k], faces[k][0])

    def halo_start(s, ks):
        for k in ks:
            @pl.when(faces[k][1])
            def _(k=k):
                halo(s, k).start()

    def halo_wait(s):
        for k in range(6):
            @pl.when(faces[k][1])
            def _(k=k):
                halo(s, k).wait_send()

            @pl.when(faces[k][2])
            def _(k=k):
                halo(s, k).wait_recv()

    lane = lax.broadcasted_iota(jnp.int32, (B, LANES), 1)
    lane_x = lane % EX
    lane_y = lane // EX

    def pack(s, load):
        def step(z, carry):
            a, b, c, d = carry
            f = load(z)
            in_y = lane_y == z
            in_x = lane_x == z
            a = jnp.where(in_y, pltpu.roll(f, EX * z, 1), a)
            b = jnp.where(in_y, pltpu.roll(f, lax.rem(EX * z + EX, LANES), 1), b)
            c = jnp.where(in_x, pltpu.roll(f, z, 1), c)
            d = jnp.where(in_x, pltpu.roll(f, lax.rem(z + LANES - EX + 1, LANES), 1), d)
            return a, b, c, d

        def loop(z, carry):
            hs = step(z, tuple(hsend[s, 2 + k] for k in range(4)))
            for k in range(4):
                hsend[s, 2 + k] = hs[k]
            return carry

        for k in range(4):
            hsend[s, 2 + k] = jnp.zeros((B, LANES), F32)
        lax.fori_loop(0, depth, loop, 0)

    half_rows = B * depth // 2
    chunk = half_rows // 8

    def first_sums(i, carry):
        a, b, c = carry
        lo = pl.ds(pl.multiple_of(i * chunk, 8), chunk)
        hi = pl.ds(pl.multiple_of(half_rows + i * chunk, 8), chunk)
        ur, ui, fr, fi = rit[lo, :], rit[hi, :], res[lo, :], res[hi, :]
        return (
            a + fold(ur * ur + ui * ui),
            b + fold(ur * fr + ui * fi),
            c + fold(ur * fi - ui * fr),
        )

    zero = jnp.zeros((8, LANES), F32)
    sums = lax.fori_loop(0, 8, first_sums, (zero, zero, zero))
    pl.semaphore_wait(barrier, G - 1 + X - 1)
    sum_start(0, *sums)

    for s, ref in ((0, res), (1, rit)):
        hsend[s, 0] = rlayer(ref, 0)
        hsend[s, 1] = rlayer(ref, depth - 1)
        halo_start(s, (0, 1))
        pack(s, functools.partial(rlayer, ref))
        halo_start(s, (2, 3, 4, 5))
    sum_middle(0)

    for k in range(6):
        @pl.when(jnp.logical_not(faces[k][2]))
        def _(k=k):
            for s in range(3):
                hrecv[s, k] = jnp.zeros((B, LANES), F32)

    fh, fl = split(jnp.concatenate([kf[n] for n in range(6)], axis=1))
    kface[0:B, :] = fh
    kface[B:2 * B, :] = fl
    ri = lax.broadcasted_iota(jnp.int32, (B, B), 0)
    ci = lax.broadcasted_iota(jnp.int32, (B, B), 1)
    half = B // 2
    shift = (
        jnp.where(ri == ci, sre[0, 0], 0.0)
        + jnp.where(ri == ci + half, sim[0, 0], 0.0)
        - jnp.where(ri + half == ci, sim[0, 0], 0.0)
    )
    for n, block in enumerate((kb[...] - shift, kr[...], kp[...])):
        bh, bl = split(block)
        kself[n * B:(n + 1) * B, :] = bh
        kself[(n + 3) * B:(n + 4) * B, :] = bl

    ci = lax.broadcasted_iota(jnp.int32, (LANES, LANES), 0)
    co = lax.broadcasted_iota(jnp.int32, (LANES, LANES), 1)
    for k in range(9):
        dy, dx = k // 3 - 1, k % 3 - 1
        oy = jnp.abs(ci // EX + EY * dy - co // EX)
        ox = jnp.abs(ci % EX + EX * dx - co % EX)
        w = jnp.maximum(REACH + 1 - oy, 0) * jnp.maximum(REACH + 1 - ox, 0)
        wlat[k * LANES:(k + 1) * LANES, :] = w.astype(F32).astype(BF16)

    def build(s, load, scale, re, im):
        def layer(z, carry):
            V[z + 1] = scale * (load(z) - removed_part(rlayer(rit, z), re, im))
            return carry

        lax.fori_loop(0, depth, layer, 0)
        halo_wait(s)
        for k in range(6):
            h = scale * (hrecv[s, k] - removed_part(hrecv[1, k], re, im))
            if k == 0:
                V[depth + 1] = h
            elif k == 1:
                V[0] = h
            else:
                H[k - 2] = h

    def image(j):
        lists = [[], [], [], [], [], [], []]
        for q in range(2):
            z = 2 * j + q
            c = V[z + 1]
            yp = jnp.where(lane_y == EY - 1, pltpu.roll(H[0], LANES - EX - EX * z, 1), pltpu.roll(c, LANES - EX, 1))
            ym = jnp.where(lane_y == 0, pltpu.roll(H[1], lax.rem(LANES - EX * z, LANES), 1), pltpu.roll(c, EX, 1))
            xp = jnp.where(lane_x == EX - 1, pltpu.roll(H[2], EX - 1 - z, 1), pltpu.roll(c, LANES - 1, 1))
            xm = jnp.where(lane_x == 0, pltpu.roll(H[3], lax.rem(LANES - z, LANES), 1), pltpu.roll(c, 1, 1))
            for entry, v in zip(lists, (c, V[z + 2], V[z], yp, ym, xp, xm)):
                entry.append(v)
        parts = [split(jnp.concatenate(e, axis=1)) for e in lists]
        fh = jnp.concatenate([p[0] for p in parts[1:]], axis=0)
        fl = jnp.concatenate([p[1] for p in parts[1:]], axis=0)
        both = mm(kface[...], fh)
        total = both[:B] + both[B:] + mm(kface[0:B, :], fl)
        ch, cl = parts[0]
        own = mm(kself[0:3 * B, :], ch) + mm(kself[3 * B:6 * B, :], ch) + mm(kself[0:3 * B, :], cl)
        d = jnp.concatenate([den[pl.ds(2 * j, 1), :], den[pl.ds(2 * j + 1, 1), :]], axis=1)
        p = jnp.concatenate([pml[pl.ds(2 * j, 1), :], pml[pl.ds(2 * j + 1, 1), :]], axis=1).astype(F32)
        rho = own[B:2 * B]
        return total + own[:B] + d * rho + p * own[2 * B:], rho

    norm, re, im = sum_end(0)
    inv = 1.0 / norm
    halo_wait(1)
    build(0, functools.partial(rlayer, res), 1.0, re * inv, im * inv)

    def apply_one(j, carry):
        a, b, c = carry
        out, unused = image(j)
        for q in range(2):
            z = 2 * j + q
            o = out[:, q * LANES:(q + 1) * LANES]
            I1[z] = o
            re_q, im_q = pair_terms(rlayer(rit, z), o)
            a, b, c = a + re_q, b + im_q, c + fold(o * o)
        return a, b, c

    sums = lax.fori_loop(0, depth // 2, apply_one, (zero, zero, zero))
    sum_start(1, *sums)
    halo_start(2, (0, 1))
    pack(2, lambda z: I1[z])
    halo_start(2, (2, 3, 4, 5))
    sum_middle(1)
    re, im, square = sum_end(1)
    factor = jnp.sqrt(count / (square - (re * re + im * im) * inv))
    build(2, lambda z: I1[z], factor, re * inv, im * inv)

    def apply_two(j, carry):
        a, b = carry
        out, rho = image(j)
        for q in range(2):
            z = 2 * j + q
            o = out[:, q * LANES:(q + 1) * LANES]
            r = rho[:, q * LANES:(q + 1) * LANES]
            I1[z] = o
            u = rlayer(rit, z)
            re_q, im_q = pair_terms(u, o)
            a, b = a + re_q, b + im_q
            w = msk[pl.ds(z, 1), :].astype(F32) * (1.0 / 36.0)
            br, bi = pair_terms(u, r)
            for n, v in enumerate((fold(o * r), br, bi)):
                sens[n, pl.ds(z, 1), :] = jnp.sum(v, axis=0, keepdims=True) * w
        return a, b

    a, b = lax.fori_loop(0, depth // 2, apply_two, (zero, zero))
    sum_start(2, a, b, zero)

    def zcopy(k):
        return remote(sens, zrecv.at[k], zss.at[k], zrs.at[k], faces[k][0])

    for k in range(2):
        @pl.when(faces[k][1])
        def _(k=k):
            zcopy(k).start()

        @pl.when(jnp.logical_not(faces[k][2]))
        def _(k=k):
            zrecv[k] = jnp.zeros((3, depth, LANES), F32)

    sum_middle(2)
    for k in range(2):
        @pl.when(faces[k][1])
        def _(k=k):
            zcopy(k).wait_send()

        @pl.when(faces[k][2])
        def _(k=k):
            zcopy(k).wait_recv()
    for n in range(3):
        zpad[n, 0:depth, :] = zrecv[1, n]
        zpad[n, depth:2 * depth, :] = sens[n]
        zpad[n, 2 * depth:3 * depth, :] = zrecv[0, n]
        total = jnp.zeros((depth, LANES), F32)
        for d in range(-REACH, REACH + 1):
            total = total + ((REACH + 1.0 - abs(d)) / 12.0) * zpad[n, depth + d:2 * depth + d, :]
        lat[n * depth:(n + 1) * depth, :] = total

    lateral = []
    for k in range(9):
        if k == 4:
            continue
        dy, dx = k // 3 - 1, k % 3 - 1
        gets = (row + dy >= 0) & (row + dy < TY) & (col + dx >= 0) & (col + dx < TX)
        gives = (row - dy >= 0) & (row - dy < TY) & (col - dx >= 0) & (col - dx < TX)
        copy = remote(lat, lrecv.at[k], lss.at[k], lrs.at[k], xy_peer(-dy * TX - dx))
        lateral.append((k, gets, gives, copy))
    for k, gets, gives, copy in lateral:
        @pl.when(gives)
        def _(copy=copy):
            copy.start()

        @pl.when(jnp.logical_not(gets))
        def _(k=k):
            lrecv[k] = jnp.zeros((3 * depth, LANES), F32)
    lrecv[4] = lat[...]

    re, im, unused = sum_end(2)
    re, im = re * inv, im * inv

    def finish(z, carry):
        cor[pl.ds(z, B, stride=depth), :] = I1[z] - removed_part(rlayer(rit, z), re, im)
        return carry

    lax.fori_loop(0, depth, finish, 0)
    for k, gets, gives, copy in lateral:
        @pl.when(gives)
        def _(copy=copy):
            copy.wait_send()

        @pl.when(gets)
        def _(copy=copy):
            copy.wait_recv()
    tiles = jnp.concatenate([lrecv[k] for k in range(9)], axis=1)
    th, tl = split(tiles)
    smooth = (mm(th, wlat[...]) + mm(tl, wlat[...])) * (1.0 / 144.0)
    fil[...] = smooth[:depth] - re * smooth[depth:2 * depth] - im * smooth[2 * depth:]


def local(G, X, residual_in, ritz_vector, density, pml_flags, design_mask, k_base, k_rho, k_pml, k_face, shift_re, shift_im):
    B, depth = residual_in.shape[:2]
    vmem = pl.BlockSpec(memory_space=pltpu.VMEM)
    smem = pl.BlockSpec(memory_space=pltpu.SMEM)
    dma = pltpu.SemaphoreType.DMA
    field = (B, LANES)
    correction, filtered = pl.pallas_call(
        functools.partial(kernel, G, X, B, depth),
        out_shape=(
            jax.ShapeDtypeStruct((B * depth, LANES), F32),
            jax.ShapeDtypeStruct((depth, LANES), F32),
        ),
        in_specs=[vmem] * 9 + [smem] * 2,
        out_specs=(vmem, vmem),
        scratch_shapes=[
            pltpu.VMEM((2 * B, 6 * B), BF16),
            pltpu.VMEM((6 * B, B), BF16),
            pltpu.VMEM((3, 6) + field, F32),
            pltpu.VMEM((3, 6) + field, F32),
            pltpu.VMEM((depth + 2,) + field, F32),
            pltpu.VMEM((4,) + field, F32),
            pltpu.VMEM((depth,) + field, F32),
            pltpu.VMEM((3, 8, LANES), F32),
            pltpu.VMEM((3, 8, LANES), F32),
            pltpu.VMEM((3, G - 1, 8, LANES), F32),
            pltpu.VMEM((3, X - 1, 8, LANES), F32),
            pltpu.VMEM((3, depth, LANES), F32),
            pltpu.VMEM((2, 3, depth, LANES), F32),
            pltpu.VMEM((3, 3 * depth, LANES), F32),
            pltpu.VMEM((3 * depth, LANES), F32),
            pltpu.VMEM((9, 3 * depth, LANES), F32),
            pltpu.VMEM((9 * LANES, LANES), BF16),
            dma((3, G - 1)),
            dma((3, G - 1)),
            dma((3, X - 1)),
            dma((3, X - 1)),
            dma((3, 6)),
            dma((3, 6)),
            dma((2,)),
            dma((2,)),
            dma((9,)),
            dma((9,)),
        ],
        compiler_params=pltpu.CompilerParams(
            collective_id=0, has_side_effects=True, vmem_limit_bytes=40 * 1024 * 1024
        ),
    )(
        residual_in.reshape(B * depth, LANES),
        ritz_vector.reshape(B * depth, LANES),
        density.reshape(depth, LANES),
        pml_flags.reshape(depth, LANES),
        design_mask.reshape(depth, LANES),
        k_base, k_rho, k_pml, k_face,
        shift_re.reshape(1, 1), shift_im.reshape(1, 1),
    )
    return correction.reshape(residual_in.shape), filtered.reshape(density.shape)


def solution(mesh):
    wide = P(None, "gz", "xy", None)
    flat = P("gz", "xy", None)
    return jax.shard_map(
        functools.partial(local, mesh.shape["gz"], mesh.shape["xy"]),
        mesh=mesh,
        in_specs=(wide, wide, flat, flat, flat, P(), P(), P(), P(), P(), P()),
        out_specs=(wide, flat),
        check_vma=False,
    )
```

profile of v0, /device:TPU:0, one launch (start us, length us, event | category | flops | bytes accessed | tf_op | source)
XLA Modules:
  0.0 48.9 jit_solution(4303694684141298191)
XLA Ops:
  1.3 0.0 copy-start.8
  1.9 0.0 copy-start.7
  2.0 0.0 copy-start.6
  2.0 0.0 copy-done.8
  2.0 0.7 %copy-done.7 = s32[8,1,128]{2,1,0:T(1,128)S(1)} copy-done((s32[8,1,128]{2,1,0:T(1,128)S(1)}, s32[8,1,128]{2,1,0:T(1,128)}, u32[]{:S(2)}) %copy-start.7) | copy-done | bytes 4120
  2.6 0.0 copy-done.6
  2.7 0.0 copy-start
  2.7 1.2 %copy-done = f32[6,144,144]{2,1,0:T(8,128)S(1)} copy-done((f32[6,144,144]{2,1,0:T(8,128)S(1)}, f32[6,144,144]{2,1,0:T(8,128)}, u32[]{:S(2)}) %copy-start) | copy-done | bytes 497688
  3.8 0.0 copy-start.1
  3.8 1.1 %copy-done.1 = f32[144,8,1,128]{3,2,1,0:T(1,128)S(1)} copy-done((f32[144,8,1,128]{3,2,1,0:T(1,128)S(1)}, f32[144,8,1,128]{3,2,1,0:T(1,128)}, u32[]{:S(2)}) %copy-start.1) | copy-done | bytes 589848
  4.9 0.0 copy-start.2
  4.9 1.1 %copy-done.2 = f32[144,8,1,128]{3,2,1,0:T(1,128)S(1)} copy-done((f32[144,8,1,128]{3,2,1,0:T(1,128)S(1)}, f32[144,8,1,128]{3,2,1,0:T(1,128)}, u32[]{:S(2)}) %copy-start.2) | copy-done | bytes 589848
  6.0 0.0 copy-start.3
  6.0 0.9 %copy-done.3 = f32[144,144]{1,0:T(8,128)S(1)} copy-done((f32[144,144]{1,0:T(8,128)S(1)}, f32[144,144]{1,0:T(8,128)}, u32[]{:S(2)}) %copy-start.3) | copy-done | bytes 82968
  6.9 0.0 copy-start.4
  6.9 0.9 %copy-done.4 = f32[144,144]{1,0:T(8,128)S(1)} copy-done((f32[144,144]{1,0:T(8,128)S(1)}, f32[144,144]{1,0:T(8,128)}, u32[]{:S(2)}) %copy-start.4) | copy-done | bytes 82968
  7.8 0.0 copy-start.5
  7.8 0.9 %copy-done.5 = f32[144,144]{1,0:T(8,128)S(1)} copy-done((f32[144,144]{1,0:T(8,128)S(1)}, f32[144,144]{1,0:T(8,128)}, u32[]{:S(2)}) %copy-start.5) | copy-done | bytes 82968
  8.7 38.8 %shard_map.122 = (f32[1152,128]{1,0:T(8,128)S(1)}, f32[8,128]{1,0:T(8,128)S(1)}) custom-call(f32[1152,128]{1,0:T(8,128)S(1)} %bitcast.16, f32[1152,128]{1,0:T(8,128)S(1)} %bitcast.17, f32[8,128]{1,0:T(8,128)S(1)} %bitcast.18, s32[8,128]{1,0:T(8,128)S(1)} %bitcast.19, s32[8,128]{1,0:T(8,128)S(1)} %bitcast.20, f32[144,144]{1,0:T(8,128)S(1)} %copy-done.3, ...), custom_call_target="tpu_custom_call" | custom-call | tf_op jit(solution)/shard_map/pallas_call | solution.py:395
  47.5 0.8 %copy.19 = f32[144,8,1,128]{3,2,1,0:T(1,128)} copy(f32[144,8,1,128]{3,2,1,0:T(1,128)S(1)} %bitcast.15) | data formatting | bytes 1179648
  48.3 0.6 %copy.20 = f32[8,1,128]{2,1,0:T(1,128)} copy(f32[8,1,128]{2,1,0:T(1,128)S(1)} %bitcast.21) | data formatting | bytes 8192
Async XLA Ops:
  1.3 0.7 %copy-start.8 = (s32[8,1,128]{2,1,0:T(1,128)S(1)}, s32[8,1,128]{2,1,0:T(1,128)}, u32[]{:S(2)}) copy-start(s32[8,1,128]{2,1,0:T(1,128)} %param.15) | copy-start | bytes 12292
  1.9 0.7 %copy-start.7 = (s32[8,1,128]{2,1,0:T(1,128)S(1)}, s32[8,1,128]{2,1,0:T(1,128)}, u32[]{:S(2)}) copy-start(s32[8,1,128]{2,1,0:T(1,128)} %param.14) | copy-start | bytes 12292
  2.0 0.7 %copy-start.6 = (f32[8,1,128]{2,1,0:T(1,128)S(1)}, f32[8,1,128]{2,1,0:T(1,128)}, u32[]{:S(2)}) copy-start(f32[8,1,128]{2,1,0:T(1,128)} %param.13) | copy-start | bytes 12292
  2.7 1.2 %copy-start = (f32[6,144,144]{2,1,0:T(8,128)S(1)}, f32[6,144,144]{2,1,0:T(8,128)}, u32[]{:S(2)}) copy-start(f32[6,144,144]{2,1,0:T(8,128)} %kf.1) | copy-start | bytes 1492996
  3.8 1.1 %copy-start.1 = (f32[144,8,1,128]{3,2,1,0:T(1,128)S(1)}, f32[144,8,1,128]{3,2,1,0:T(1,128)}, u32[]{:S(2)}) copy-start(f32[144,8,1,128]{3,2,1,0:T(1,128)} %param.11) | copy-start | bytes 1769476
  4.9 1.1 %copy-start.2 = (f32[144,8,1,128]{3,2,1,0:T(1,128)S(1)}, f32[144,8,1,128]{3,2,1,0:T(1,128)}, u32[]{:S(2)}) copy-start(f32[144,8,1,128]{3,2,1,0:T(1,128)} %param.12) | copy-start | bytes 1769476
  6.0 0.9 %copy-start.3 = (f32[144,144]{1,0:T(8,128)S(1)}, f32[144,144]{1,0:T(8,128)}, u32[]{:S(2)}) copy-start(f32[144,144]{1,0:T(8,128)} %kb.1) | copy-start | bytes 248836
  6.9 0.9 %copy-start.4 = (f32[144,144]{1,0:T(8,128)S(1)}, f32[144,144]{1,0:T(8,128)}, u32[]{:S(2)}) copy-start(f32[144,144]{1,0:T(8,128)} %kr.1) | copy-start | bytes 248836
  7.8 0.9 %copy-start.5 = (f32[144,144]{1,0:T(8,128)S(1)}, f32[144,144]{1,0:T(8,128)}, u32[]{:S(2)}) copy-start(f32[144,144]{1,0:T(8,128)} %kp.1) | copy-start | bytes 248836
where the time goes:
time: 49.3 us; the launch traced here: 48.9 us
  Pallas kernels  38.8 us (79%)
  local copies, waits for them, and re-layouts  8.11 us (16%)
  between operations  1.99 us (4%)
    pallas_call x1, Pallas kernels, local(): pl.pallas_call(functools.partial(kernel, G, X, B, depth), out_shape=(jax....  38.8 us
    unnamed x20, local copies, waits for them, and re-layouts  8.11 us

commit v1 on v0

--- a/solution.py
+++ b/solution.py
@@ -44,11 +44,12 @@
 
 def kernel(
     G, X, B, depth,
-    res, rit, den, pml, msk, kb, kr, kp, kf, sre, sim,
+    res_in, rit_in, den_in, pml_in, msk_in, kb_in, kr_in, kp_in, kf_in, sre, sim,
     cor, fil,
-    kface, kself, hsend, hrecv, V, H, I1, st, st2, p1, p2,
+    res, rit, den, pml, msk, kb, kr, kp, kf,
+    kface, kedge, kself, hsend, hrecv, edge, V, I1, RHO, st, st2, p1, p2,
     sens, zrecv, zpad, lat, lrecv, wlat,
-    s1s, s1r, s2s, s2r, hss, hrs, zss, zrs, lss, lrs,
+    ins, s1s, s1r, s2s, s2r, hss, hrs, zss, zrs, lss, lrs,
 ):
     g = lax.axis_index("gz")
     t = lax.axis_index("xy")
@@ -56,6 +57,16 @@
     row = t // TX
     TY = X // TX
     count = float(B * depth * LANES * G * X)
+
+    loads = [
+        pltpu.make_async_copy(src, dst, ins.at[n])
+        for n, (src, dst) in enumerate((
+            (rit_in, rit), (res_in, res), (kf_in, kf), (kb_in, kb), (kr_in, kr), (kp_in, kp),
+            (den_in, den), (pml_in, pml), (msk_in, msk),
+        ))
+    ]
+    for copy in loads:
+        copy.start()
 
     def gz_peer(o):
         return {"gz": lax.rem(g + o + G, G)}
@@ -125,9 +136,7 @@
     ]
 
     def halo(s, k):
-        src = hsend.at[s, k]
-        if s == 2 and k < 2:
-            src = I1.at[0 if k == 0 else depth - 1]
+        src = (V.at[1], V.at[depth])[k] if k < 2 else hsend.at[s, k - 2]
         return remote(src, hrecv.at[s, k], hss.at[s, k], hrs.at[s, k], faces[k][0])
 
     def halo_start(s, ks):
@@ -150,27 +159,17 @@
     lane_x = lane % EX
     lane_y = lane // EX
 
-    def pack(s, load):
-        def step(z, carry):
-            a, b, c, d = carry
-            f = load(z)
-            in_y = lane_y == z
-            in_x = lane_x == z
-            a = jnp.where(in_y, pltpu.roll(f, EX * z, 1), a)
-            b = jnp.where(in_y, pltpu.roll(f, lax.rem(EX * z + EX, LANES), 1), b)
-            c = jnp.where(in_x, pltpu.roll(f, z, 1), c)
-            d = jnp.where(in_x, pltpu.roll(f, lax.rem(z + LANES - EX + 1, LANES), 1), d)
-            return a, b, c, d
-
-        def loop(z, carry):
-            hs = step(z, tuple(hsend[s, 2 + k] for k in range(4)))
-            for k in range(4):
-                hsend[s, 2 + k] = hs[k]
-            return carry
-
-        for k in range(4):
-            hsend[s, 2 + k] = jnp.zeros((B, LANES), F32)
-        lax.fori_loop(0, depth, loop, 0)
+    def pack(s, z, f):
+        in_y = lane_y == z
+        in_x = lane_x == z
+        turned = (
+            (in_y, pltpu.roll(f, EX * z, 1)),
+            (in_y, pltpu.roll(f, lax.rem(EX * z + EX, LANES), 1)),
+            (in_x, pltpu.roll(f, z, 1)),
+            (in_x, pltpu.roll(f, lax.rem(z + LANES - EX + 1, LANES), 1)),
+        )
+        for k, (where, v) in enumerate(turned):
+            hsend[s, k] = jnp.where(where, v, hsend[s, k])
 
     half_rows = B * depth // 2
     chunk = half_rows // 8
@@ -187,27 +186,35 @@
         )
 
     zero = jnp.zeros((8, LANES), F32)
+    loads[0].wait()
+    loads[1].wait()
     sums = lax.fori_loop(0, 8, first_sums, (zero, zero, zero))
     pl.semaphore_wait(barrier, G - 1 + X - 1)
     sum_start(0, *sums)
 
-    for s, ref in ((0, res), (1, rit)):
-        hsend[s, 0] = rlayer(ref, 0)
-        hsend[s, 1] = rlayer(ref, depth - 1)
-        halo_start(s, (0, 1))
-        pack(s, functools.partial(rlayer, ref))
-        halo_start(s, (2, 3, 4, 5))
-    sum_middle(0)
-
+    blank = jnp.zeros((B, LANES), F32)
+    for s in range(2):
+        for k in range(4):
+            hsend[s, k] = blank
+    V[0] = blank
+    V[depth + 1] = blank
     for k in range(6):
         @pl.when(jnp.logical_not(faces[k][2]))
         def _(k=k):
-            for s in range(3):
-                hrecv[s, k] = jnp.zeros((B, LANES), F32)
+            for s in range(2):
+                hrecv[s, k] = blank
+
+    for copy in loads[2:]:
+        copy.wait()
 
     fh, fl = split(jnp.concatenate([kf[n] for n in range(6)], axis=1))
     kface[0:B, :] = fh
     kface[B:2 * B, :] = fl
+    sum_middle(0)
+    for n in range(6):
+        bh, bl = split(kf[n])
+        kedge[n, 0:B, :] = bh
+        kedge[n, B:2 * B, :] = bl
     ri = lax.broadcasted_iota(jnp.int32, (B, B), 0)
     ci = lax.broadcasted_iota(jnp.int32, (B, B), 1)
     half = B // 2
@@ -232,29 +239,41 @@
 
     def build(s, load, scale, re, im):
         def layer(z, carry):
-            V[z + 1] = scale * (load(z) - removed_part(rlayer(rit, z), re, im))
+            v = scale * (load(z) - removed_part(rlayer(rit, z), re, im))
+            V[z + 1] = v
+            pack(s, z, v)
             return carry
 
         lax.fori_loop(0, depth, layer, 0)
+        halo_start(s, range(6))
+
+    def rims(s):
         halo_wait(s)
         for k in range(6):
-            h = scale * (hrecv[s, k] - removed_part(hrecv[1, k], re, im))
-            if k == 0:
-                V[depth + 1] = h
-            elif k == 1:
-                V[0] = h
-            else:
-                H[k - 2] = h
+            hh, hl = split(hrecv[s, k])
+            both = mm(kedge[k], hh)
+            edge[k] = both[:B] + both[B:] + mm(kedge[k, 0:B, :], hl)
+        I1[depth - 1] += edge[0]
+        I1[0] += edge[1]
+
+    def with_rims(z):
+        return (
+            I1[z]
+            + jnp.where(lane_y == EY - 1, pltpu.roll(edge[2], LANES - EX - EX * z, 1), 0.0)
+            + jnp.where(lane_y == 0, pltpu.roll(edge[3], lax.rem(LANES - EX * z, LANES), 1), 0.0)
+            + jnp.where(lane_x == EX - 1, pltpu.roll(edge[4], EX - 1 - z, 1), 0.0)
+            + jnp.where(lane_x == 0, pltpu.roll(edge[5], lax.rem(LANES - z, LANES), 1), 0.0)
+        )
 
     def image(j):
         lists = [[], [], [], [], [], [], []]
         for q in range(2):
             z = 2 * j + q
             c = V[z + 1]
-            yp = jnp.where(lane_y == EY - 1, pltpu.roll(H[0], LANES - EX - EX * z, 1), pltpu.roll(c, LANES - EX, 1))
-            ym = jnp.where(lane_y == 0, pltpu.roll(H[1], lax.rem(LANES - EX * z, LANES), 1), pltpu.roll(c, EX, 1))
-            xp = jnp.where(lane_x == EX - 1, pltpu.roll(H[2], EX - 1 - z, 1), pltpu.roll(c, LANES - 1, 1))
-            xm = jnp.where(lane_x == 0, pltpu.roll(H[3], lax.rem(LANES - z, LANES), 1), pltpu.roll(c, 1, 1))
+            yp = jnp.where(lane_y == EY - 1, 0.0, pltpu.roll(c, LANES - EX, 1))
+            ym = jnp.where(lane_y == 0, 0.0, pltpu.roll(c, EX, 1))
+            xp = jnp.where(lane_x == EX - 1, 0.0, pltpu.roll(c, LANES - 1, 1))
+            xm = jnp.where(lane_x == 0, 0.0, pltpu.roll(c, 1, 1))
             for entry, v in zip(lists, (c, V[z + 2], V[z], yp, ym, xp, xm)):
                 entry.append(v)
         parts = [split(jnp.concatenate(e, axis=1)) for e in lists]
@@ -267,52 +286,57 @@
         d = jnp.concatenate([den[pl.ds(2 * j, 1), :], den[pl.ds(2 * j + 1, 1), :]], axis=1)
         p = jnp.concatenate([pml[pl.ds(2 * j, 1), :], pml[pl.ds(2 * j + 1, 1), :]], axis=1).astype(F32)
         rho = own[B:2 * B]
-        return total + own[:B] + d * rho + p * own[2 * B:], rho
+        out = total + own[:B] + d * rho + p * own[2 * B:]
+        for q in range(2):
+            I1[2 * j + q] = out[:, q * LANES:(q + 1) * LANES]
+        return rho
 
     norm, re, im = sum_end(0)
     inv = 1.0 / norm
-    halo_wait(1)
     build(0, functools.partial(rlayer, res), 1.0, re * inv, im * inv)
 
     def apply_one(j, carry):
+        image(j)
+        return carry
+
+    def sums_one(z, carry):
         a, b, c = carry
-        out, unused = image(j)
-        for q in range(2):
-            z = 2 * j + q
-            o = out[:, q * LANES:(q + 1) * LANES]
-            I1[z] = o
-            re_q, im_q = pair_terms(rlayer(rit, z), o)
-            a, b, c = a + re_q, b + im_q, c + fold(o * o)
-        return a, b, c
-
-    sums = lax.fori_loop(0, depth // 2, apply_one, (zero, zero, zero))
+        o = with_rims(z)
+        I1[z] = o
+        re_z, im_z = pair_terms(rlayer(rit, z), o)
+        return a + re_z, b + im_z, c + fold(o * o)
+
+    lax.fori_loop(0, depth // 2, apply_one, 0)
+    rims(0)
+    sums = lax.fori_loop(0, depth, sums_one, (zero, zero, zero))
     sum_start(1, *sums)
-    halo_start(2, (0, 1))
-    pack(2, lambda z: I1[z])
-    halo_start(2, (2, 3, 4, 5))
     sum_middle(1)
     re, im, square = sum_end(1)
     factor = jnp.sqrt(count / (square - (re * re + im * im) * inv))
-    build(2, lambda z: I1[z], factor, re * inv, im * inv)
+    build(1, lambda z: I1[z], factor, re * inv, im * inv)
 
     def apply_two(j, carry):
+        rho = image(j)
+        for q in range(2):
+            RHO[2 * j + q] = rho[:, q * LANES:(q + 1) * LANES]
+        return carry
+
+    def sums_two(z, carry):
         a, b = carry
-        out, rho = image(j)
-        for q in range(2):
-            z = 2 * j + q
-            o = out[:, q * LANES:(q + 1) * LANES]
-            r = rho[:, q * LANES:(q + 1) * LANES]
-            I1[z] = o
-            u = rlayer(rit, z)
-            re_q, im_q = pair_terms(u, o)
-            a, b = a + re_q, b + im_q
-            w = msk[pl.ds(z, 1), :].astype(F32) * (1.0 / 36.0)
-            br, bi = pair_terms(u, r)
-            for n, v in enumerate((fold(o * r), br, bi)):
-                sens[n, pl.ds(z, 1), :] = jnp.sum(v, axis=0, keepdims=True) * w
-        return a, b
-
-    a, b = lax.fori_loop(0, depth // 2, apply_two, (zero, zero))
+        o = with_rims(z)
+        I1[z] = o
+        r = RHO[z]
+        u = rlayer(rit, z)
+        re_z, im_z = pair_terms(u, o)
+        w = msk[pl.ds(z, 1), :].astype(F32) * (1.0 / 36.0)
+        br, bi = pair_terms(u, r)
+        for n, v in enumerate((fold(o * r), br, bi)):
+            sens[n, pl.ds(z, 1), :] = jnp.sum(v, axis=0, keepdims=True) * w
+        return a + re_z, b + im_z
+
+    lax.fori_loop(0, depth // 2, apply_two, 0)
+    rims(1)
+    a, b = lax.fori_loop(0, depth, sums_two, (zero, zero))
     sum_start(2, a, b, zero)
 
     def zcopy(k):
@@ -398,15 +422,26 @@
             jax.ShapeDtypeStruct((B * depth, LANES), F32),
             jax.ShapeDtypeStruct((depth, LANES), F32),
         ),
-        in_specs=[vmem] * 9 + [smem] * 2,
+        in_specs=[pl.BlockSpec(memory_space=pltpu.HBM)] * 9 + [smem] * 2,
         out_specs=(vmem, vmem),
         scratch_shapes=[
+            pltpu.VMEM((B * depth, LANES), F32),
+            pltpu.VMEM((B * depth, LANES), F32),
+            pltpu.VMEM((depth, LANES), F32),
+            pltpu.VMEM((depth, LANES), jnp.int32),
+            pltpu.VMEM((depth, LANES), jnp.int32),
+            pltpu.VMEM((B, B), F32),
+            pltpu.VMEM((B, B), F32),
+            pltpu.VMEM((B, B), F32),
+            pltpu.VMEM((6, B, B), F32),
             pltpu.VMEM((2 * B, 6 * B), BF16),
+            pltpu.VMEM((6, 2 * B, B), BF16),
             pltpu.VMEM((6 * B, B), BF16),
-            pltpu.VMEM((3, 6) + field, F32),
-            pltpu.VMEM((3, 6) + field, F32),
+            pltpu.VMEM((2, 4) + field, F32),
+            pltpu.VMEM((2, 6) + field, F32),
+            pltpu.VMEM((6,) + field, F32),
             pltpu.VMEM((depth + 2,) + field, F32),
-            pltpu.VMEM((4,) + field, F32),
+            pltpu.VMEM((depth,) + field, F32),
             pltpu.VMEM((depth,) + field, F32),
             pltpu.VMEM((3, 8, LANES), F32),
             pltpu.VMEM((3, 8, LANES), F32),
@@ -418,19 +453,20 @@
             pltpu.VMEM((3 * depth, LANES), F32),
             pltpu.VMEM((9, 3 * depth, LANES), F32),
             pltpu.VMEM((9 * LANES, LANES), BF16),
+            dma((9,)),
             dma((3, G - 1)),
             dma((3, G - 1)),
             dma((3, X - 1)),
             dma((3, X - 1)),
-            dma((3, 6)),
-            dma((3, 6)),
+            dma((2, 6)),
+            dma((2, 6)),
             dma((2,)),
             dma((2,)),
             dma((9,)),
             dma((9,)),
         ],
         compiler_params=pltpu.CompilerParams(
-            collective_id=0, has_side_effects=True, vmem_limit_bytes=40 * 1024 * 1024
+            collective_id=0, has_side_effects=True, vmem_limit_bytes=64 * 1024 * 1024
         ),
     )(
         residual_in.reshape(B * depth, LANES),

time: 49.3 us -> 50.1 us (1.016)
  Pallas kernels: 38.8 us -> 45.1 us
  local copies, waits for them, and re-layouts: 8.11 us -> 2.88 us
    pallas_call x1, Pallas kernels: 38.8 us -> 45.1 us  [local(): pl.pallas_call(functools.partial(kernel, G, X, B, depth), out_shape=(jax....]
    unnamed x20 -> x4, local copies, waits for them, and re-layouts: 8.11 us -> 2.88 us
where the time goes in v1:
time: 50.1 us; the launch traced here: 49.9 us
  Pallas kernels  45.1 us (90%)
  local copies, waits for them, and re-layouts  2.88 us (6%)
  between operations  1.94 us (4%)
    pallas_call x1, Pallas kernels, local(): pl.pallas_call(functools.partial(kernel, G, X, B, depth), out_shape=(jax....  45.1 us
    unnamed x4, local copies, waits for them, and re-layouts  2.88 us

profile of v1, /device:TPU:0, one launch (start us, length us, event | category | flops | bytes accessed | tf_op | source)
XLA Modules:
  0.0 49.9 jit_solution(12607070101740041042)
XLA Ops:
  1.9 45.1 %shard_map.122 = (f32[1152,128]{1,0:T(8,128)}, f32[8,128]{1,0:T(8,128)}) custom-call(f32[1152,128]{1,0:T(8,128)} %bitcast.16, f32[1152,128]{1,0:T(8,128)} %bitcast.17, f32[8,128]{1,0:T(8,128)} %bitcast.18, s32[8,128]{1,0:T(8,128)} %bitcast.19, s32[8,128]{1,0:T(8,128)} %bitcast.20, f32[144,144]{1,0:T(8,128)} %kb_in.1, f32[144,144]{1,0:T(8,128)} %kr_in.1, ...), custom_call_target="tpu_custom_call" | custom-call | tf_op jit(solution)/shard_map/pallas_call | solution.py:419
  47.0 0.0 copy-start
  47.0 2.3 %copy.19 = f32[144,8,1,128]{3,2,1,0:T(1,128)} copy(f32[144,8,1,128]{3,2,1,0:T(1,128)} %bitcast.15) | data formatting | bytes 1179648
  49.3 0.0 copy-done
  49.3 0.6 %copy.20 = f32[8,1,128]{2,1,0:T(1,128)} copy(f32[8,1,128]{2,1,0:T(1,128)S(1)} %bitcast.21) | data formatting | bytes 8192
Async XLA Ops:
  47.0 2.3 %copy-start = (f32[8,128]{1,0:T(8,128)S(1)}, f32[8,128]{1,0:T(8,128)}, u32[]{:S(2)}) copy-start(f32[8,128]{1,0:T(8,128)} %get-tuple-element.5) | copy-start | bytes 12292

commit v2 on v0

--- a/solution.py
+++ b/solution.py
@@ -44,11 +44,12 @@
 
 def kernel(
     G, X, B, depth,
-    res, rit, den, pml, msk, kb, kr, kp, kf, sre, sim,
+    res_in, rit_in, den_in, pml_in, msk_in, kb_in, kr_in, kp_in, kf_in, sre, sim,
     cor, fil,
+    res, rit, den, pml, msk, kb, kr, kp, kf, R, U,
     kface, kself, hsend, hrecv, V, H, I1, st, st2, p1, p2,
     sens, zrecv, zpad, lat, lrecv, wlat,
-    s1s, s1r, s2s, s2r, hss, hrs, zss, zrs, lss, lrs,
+    ins, s1s, s1r, s2s, s2r, hss, hrs, zss, zrs, lss, lrs,
 ):
     g = lax.axis_index("gz")
     t = lax.axis_index("xy")
@@ -56,6 +57,16 @@
     row = t // TX
     TY = X // TX
     count = float(B * depth * LANES * G * X)
+
+    loads = [
+        pltpu.make_async_copy(src, dst, ins.at[n])
+        for n, (src, dst) in enumerate((
+            (rit_in, rit), (res_in, res), (kf_in, kf), (kb_in, kb), (kr_in, kr), (kp_in, kp),
+            (den_in, den), (pml_in, pml), (msk_in, msk),
+        ))
+    ]
+    for copy in loads:
+        copy.start()
 
     def gz_peer(o):
         return {"gz": lax.rem(g + o + G, G)}
@@ -125,9 +136,7 @@
     ]
 
     def halo(s, k):
-        src = hsend.at[s, k]
-        if s == 2 and k < 2:
-            src = I1.at[0 if k == 0 else depth - 1]
+        src = (R, U, I1)[s].at[(0, depth - 1)[k]] if k < 2 else hsend.at[s, k - 2]
         return remote(src, hrecv.at[s, k], hss.at[s, k], hrs.at[s, k], faces[k][0])
 
     def halo_start(s, ks):
@@ -146,7 +155,7 @@
             def _(k=k):
                 halo(s, k).wait_recv()
 
-    lane = lax.broadcasted_iota(jnp.int32, (B, LANES), 1)
+    lane = lax.broadcasted_iota(jnp.int32, (1, LANES), 1)
     lane_x = lane % EX
     lane_y = lane // EX
 
@@ -163,13 +172,13 @@
             return a, b, c, d
 
         def loop(z, carry):
-            hs = step(z, tuple(hsend[s, 2 + k] for k in range(4)))
+            hs = step(z, tuple(hsend[s, k] for k in range(4)))
             for k in range(4):
-                hsend[s, 2 + k] = hs[k]
+                hsend[s, k] = hs[k]
             return carry
 
         for k in range(4):
-            hsend[s, 2 + k] = jnp.zeros((B, LANES), F32)
+            hsend[s, k] = jnp.zeros((B, LANES), F32)
         lax.fori_loop(0, depth, loop, 0)
 
     half_rows = B * depth // 2
@@ -187,17 +196,30 @@
         )
 
     zero = jnp.zeros((8, LANES), F32)
+    loads[0].wait()
+    loads[1].wait()
     sums = lax.fori_loop(0, 8, first_sums, (zero, zero, zero))
     pl.semaphore_wait(barrier, G - 1 + X - 1)
     sum_start(0, *sums)
 
-    for s, ref in ((0, res), (1, rit)):
-        hsend[s, 0] = rlayer(ref, 0)
-        hsend[s, 1] = rlayer(ref, depth - 1)
+    for s, ref, layers in ((0, res, R), (1, rit, U)):
+        for k, z in ((0, 0), (1, depth - 1)):
+            layers[z] = rlayer(ref, z)
         halo_start(s, (0, 1))
-        pack(s, functools.partial(rlayer, ref))
+
+        def turned(z, ref=ref, layers=layers):
+            f = rlayer(ref, z)
+
+            @pl.when((z > 0) & (z < depth - 1))
+            def _():
+                layers[z] = f
+
+            return f
+
+        pack(s, turned)
         halo_start(s, (2, 3, 4, 5))
-    sum_middle(0)
+        if s == 0:
+            sum_middle(0)
 
     for k in range(6):
         @pl.when(jnp.logical_not(faces[k][2]))
@@ -205,6 +227,8 @@
             for s in range(3):
                 hrecv[s, k] = jnp.zeros((B, LANES), F32)
 
+    for copy in loads[2:]:
+        copy.wait()
     fh, fl = split(jnp.concatenate([kf[n] for n in range(6)], axis=1))
     kface[0:B, :] = fh
     kface[B:2 * B, :] = fl
@@ -217,9 +241,8 @@
         - jnp.where(ri + half == ci, sim[0, 0], 0.0)
     )
     for n, block in enumerate((kb[...] - shift, kr[...], kp[...])):
-        bh, bl = split(block)
-        kself[n * B:(n + 1) * B, :] = bh
-        kself[(n + 3) * B:(n + 4) * B, :] = bl
+        bh, bl = (v.astype(F32) for v in split(block))
+        kself[n * B:(n + 1) * B, :] = jnp.concatenate([bh, bh, bl], axis=1).astype(BF16)
 
     ci = lax.broadcasted_iota(jnp.int32, (LANES, LANES), 0)
     co = lax.broadcasted_iota(jnp.int32, (LANES, LANES), 1)
@@ -232,7 +255,7 @@
 
     def build(s, load, scale, re, im):
         def layer(z, carry):
-            V[z + 1] = scale * (load(z) - removed_part(rlayer(rit, z), re, im))
+            V[z + 1] = scale * (load(z) - removed_part(U[z], re, im))
             return carry
 
         lax.fori_loop(0, depth, layer, 0)
@@ -263,7 +286,7 @@
         both = mm(kface[...], fh)
         total = both[:B] + both[B:] + mm(kface[0:B, :], fl)
         ch, cl = parts[0]
-        own = mm(kself[0:3 * B, :], ch) + mm(kself[3 * B:6 * B, :], ch) + mm(kself[0:3 * B, :], cl)
+        own = mm(kself[...], jnp.concatenate([ch, cl, ch], axis=0))
         d = jnp.concatenate([den[pl.ds(2 * j, 1), :], den[pl.ds(2 * j + 1, 1), :]], axis=1)
         p = jnp.concatenate([pml[pl.ds(2 * j, 1), :], pml[pl.ds(2 * j + 1, 1), :]], axis=1).astype(F32)
         rho = own[B:2 * B]
@@ -272,7 +295,7 @@
     norm, re, im = sum_end(0)
     inv = 1.0 / norm
     halo_wait(1)
-    build(0, functools.partial(rlayer, res), 1.0, re * inv, im * inv)
+    build(0, lambda z: R[z], 1.0, re * inv, im * inv)
 
     def apply_one(j, carry):
         a, b, c = carry
@@ -281,7 +304,7 @@
             z = 2 * j + q
             o = out[:, q * LANES:(q + 1) * LANES]
             I1[z] = o
-            re_q, im_q = pair_terms(rlayer(rit, z), o)
+            re_q, im_q = pair_terms(U[z], o)
             a, b, c = a + re_q, b + im_q, c + fold(o * o)
         return a, b, c
 
@@ -303,7 +326,7 @@
             o = out[:, q * LANES:(q + 1) * LANES]
             r = rho[:, q * LANES:(q + 1) * LANES]
             I1[z] = o
-            u = rlayer(rit, z)
+            u = U[z]
             re_q, im_q = pair_terms(u, o)
             a, b = a + re_q, b + im_q
             w = msk[pl.ds(z, 1), :].astype(F32) * (1.0 / 36.0)
@@ -368,7 +391,7 @@
     re, im = re * inv, im * inv
 
     def finish(z, carry):
-        cor[pl.ds(z, B, stride=depth), :] = I1[z] - removed_part(rlayer(rit, z), re, im)
+        cor[pl.ds(z, B, stride=depth), :] = I1[z] - removed_part(U[z], re, im)
         return carry
 
     lax.fori_loop(0, depth, finish, 0)
@@ -395,15 +418,26 @@
     correction, filtered = pl.pallas_call(
         functools.partial(kernel, G, X, B, depth),
         out_shape=(
-            jax.ShapeDtypeStruct((B * depth, LANES), F32),
-            jax.ShapeDtypeStruct((depth, LANES), F32),
+            pltpu.VMEM((B * depth, LANES), F32),
+            pltpu.VMEM((depth, LANES), F32),
         ),
-        in_specs=[vmem] * 9 + [smem] * 2,
+        in_specs=[pl.BlockSpec(memory_space=pltpu.HBM)] * 9 + [smem] * 2,
         out_specs=(vmem, vmem),
         scratch_shapes=[
+            pltpu.VMEM((B * depth, LANES), F32),
+            pltpu.VMEM((B * depth, LANES), F32),
+            pltpu.VMEM((depth, LANES), F32),
+            pltpu.VMEM((depth, LANES), jnp.int32),
+            pltpu.VMEM((depth, LANES), jnp.int32),
+            pltpu.VMEM((B, B), F32),
+            pltpu.VMEM((B, B), F32),
+            pltpu.VMEM((B, B), F32),
+            pltpu.VMEM((6, B, B), F32),
+            pltpu.VMEM((depth,) + field, F32),
+            pltpu.VMEM((depth,) + field, F32),
             pltpu.VMEM((2 * B, 6 * B), BF16),
-            pltpu.VMEM((6 * B, B), BF16),
-            pltpu.VMEM((3, 6) + field, F32),
+            pltpu.VMEM((3 * B, 3 * B), BF16),
+            pltpu.VMEM((3, 4) + field, F32),
             pltpu.VMEM((3, 6) + field, F32),
             pltpu.VMEM((depth + 2,) + field, F32),
             pltpu.VMEM((4,) + field, F32),
@@ -418,6 +452,7 @@
             pltpu.VMEM((3 * depth, LANES), F32),
             pltpu.VMEM((9, 3 * depth, LANES), F32),
             pltpu.VMEM((9 * LANES, LANES), BF16),
+            dma((9,)),
             dma((3, G - 1)),
             dma((3, G - 1)),
             dma((3, X - 1)),
@@ -433,12 +468,17 @@
             collective_id=0, has_side_effects=True, vmem_limit_bytes=40 * 1024 * 1024
         ),
     )(
-        residual_in.reshape(B * depth, LANES),
-        ritz_vector.reshape(B * depth, LANES),
-        density.reshape(depth, LANES),
-        pml_flags.reshape(depth, LANES),
-        design_mask.reshape(depth, LANES),
-        k_base, k_rho, k_pml, k_face,
+        *(
+            pltpu.with_memory_space_constraint(x, pltpu.HBM)
+            for x in (
+                residual_in.reshape(B * depth, LANES),
+                ritz_vector.reshape(B * depth, LANES),
+                density.reshape(depth, LANES),
+                pml_flags.reshape(depth, LANES),
+                design_mask.reshape(depth, LANES),
+                k_base, k_rho, k_pml, k_face,
+            )
+        ),
         shift_re.reshape(1, 1), shift_im.reshape(1, 1),
     )
     return correction.reshape(residual_in.shape), filtered.reshape(density.shape)

time: 49.3 us -> 42.2 us (0.86)
  local copies, waits for them, and re-layouts: 8.11 us -> 1.41 us
    unnamed x20 -> x2, local copies, waits for them, and re-layouts: 8.11 us -> 1.41 us
where the time goes in v2:
time: 42.2 us; the launch traced here: 42.1 us
  Pallas kernels  38.7 us (92%)
  between operations  1.93 us (5%)
  local copies, waits for them, and re-layouts  1.41 us (3%)
    pallas_call x1, Pallas kernels, local(): pl.pallas_call(functools.partial(kernel, G, X, B, depth), out_shape=(pltp...  38.7 us
    unnamed x2, local copies, waits for them, and re-layouts  1.41 us

profile of v2, /device:TPU:0, one launch (start us, length us, event | category | flops | bytes accessed | tf_op | source)
XLA Modules:
  0.0 42.1 jit_solution(4731454400209428691)
XLA Ops:
  1.9 38.7 %shard_map.122 = (f32[1152,128]{1,0:T(8,128)S(1)}, f32[8,128]{1,0:T(8,128)S(1)}) custom-call(f32[1152,128]{1,0:T(8,128)} %bitcast.17, f32[1152,128]{1,0:T(8,128)} %bitcast.18, f32[8,128]{1,0:T(8,128)} %bitcast.19, s32[8,128]{1,0:T(8,128)} %bitcast.20, s32[8,128]{1,0:T(8,128)} %bitcast.21, f32[144,144]{1,0:T(8,128)} %kb_in.1, f32[144,144]{1,0:T(8,128)} %kr_in.1, ...), custom_call_target="tpu_custom_call" | custom-call | tf_op jit(solution)/shard_map/pallas_call | solution.py:418
  40.7 0.8 %copy.17 = f32[144,8,1,128]{3,2,1,0:T(1,128)} copy(f32[144,8,1,128]{3,2,1,0:T(1,128)S(1)} %bitcast.15) | data formatting | bytes 1179648
  41.5 0.6 %copy.18 = f32[8,1,128]{2,1,0:T(1,128)} copy(f32[8,1,128]{2,1,0:T(1,128)S(1)} %bitcast.16) | data formatting | bytes 8192

commit v3 on v2

--- a/solution.py
+++ b/solution.py
@@ -217,9 +217,9 @@
             return f
 
         pack(s, turned)
-        halo_start(s, (2, 3, 4, 5))
         if s == 0:
             sum_middle(0)
+        halo_start(s, (2, 3, 4, 5))
 
     for k in range(6):
         @pl.when(jnp.logical_not(faces[k][2]))
@@ -312,8 +312,8 @@
     sum_start(1, *sums)
     halo_start(2, (0, 1))
     pack(2, lambda z: I1[z])
+    sum_middle(1)
     halo_start(2, (2, 3, 4, 5))
-    sum_middle(1)
     re, im, square = sum_end(1)
     factor = jnp.sqrt(count / (square - (re * re + im * im) * inv))
     build(2, lambda z: I1[z], factor, re * inv, im * inv)

time: 42.2 us -> 43.2 us (1.024)
  Pallas kernels: 38.7 us -> 39.7 us
    pallas_call x1, Pallas kernels: 38.7 us -> 39.7 us  [local(): pl.pallas_call(functools.partial(kernel, G, X, B, depth), out_shape=(pltp...]
where the time goes in v3:
time: 43.2 us; the launch traced here: 43.1 us
  Pallas kernels  39.7 us (92%)
  between operations  1.93 us (4%)
  local copies, waits for them, and re-layouts  1.41 us (3%)
    pallas_call x1, Pallas kernels, local(): pl.pallas_call(functools.partial(kernel, G, X, B, depth), out_shape=(pltp...  39.7 us
    unnamed x2, local copies, waits for them, and re-layouts  1.41 us

profile of v3, /device:TPU:0, one launch (start us, length us, event | category | flops | bytes accessed | tf_op | source)
XLA Modules:
  0.0 43.1 jit_solution(7910076627796040375)
XLA Ops:
  1.9 39.7 %shard_map.122 = (f32[1152,128]{1,0:T(8,128)S(1)}, f32[8,128]{1,0:T(8,128)S(1)}) custom-call(f32[1152,128]{1,0:T(8,128)} %bitcast.17, f32[1152,128]{1,0:T(8,128)} %bitcast.18, f32[8,128]{1,0:T(8,128)} %bitcast.19, s32[8,128]{1,0:T(8,128)} %bitcast.20, s32[8,128]{1,0:T(8,128)} %bitcast.21, f32[144,144]{1,0:T(8,128)} %kb_in.1, f32[144,144]{1,0:T(8,128)} %kr_in.1, ...), custom_call_target="tpu_custom_call" | custom-call | tf_op jit(solution)/shard_map/pallas_call | solution.py:418
  41.6 0.8 %copy.17 = f32[144,8,1,128]{3,2,1,0:T(1,128)} copy(f32[144,8,1,128]{3,2,1,0:T(1,128)S(1)} %bitcast.15) | data formatting | bytes 1179648
  42.5 0.6 %copy.18 = f32[8,1,128]{2,1,0:T(1,128)} copy(f32[8,1,128]{2,1,0:T(1,128)S(1)} %bitcast.16) | data formatting | bytes 8192

commit v4 on v3

--- a/solution.py
+++ b/solution.py
@@ -159,67 +159,43 @@
     lane_x = lane % EX
     lane_y = lane // EX
 
-    def pack(s, load):
-        def step(z, carry):
-            a, b, c, d = carry
-            f = load(z)
-            in_y = lane_y == z
-            in_x = lane_x == z
-            a = jnp.where(in_y, pltpu.roll(f, EX * z, 1), a)
-            b = jnp.where(in_y, pltpu.roll(f, lax.rem(EX * z + EX, LANES), 1), b)
-            c = jnp.where(in_x, pltpu.roll(f, z, 1), c)
-            d = jnp.where(in_x, pltpu.roll(f, lax.rem(z + LANES - EX + 1, LANES), 1), d)
-            return a, b, c, d
-
-        def loop(z, carry):
-            hs = step(z, tuple(hsend[s, k] for k in range(4)))
-            for k in range(4):
-                hsend[s, k] = hs[k]
-            return carry
-
+    def pack(s, z, f):
+        in_y = lane_y == z
+        in_x = lane_x == z
+        turned = (
+            (in_y, pltpu.roll(f, EX * z, 1)),
+            (in_y, pltpu.roll(f, lax.rem(EX * z + EX, LANES), 1)),
+            (in_x, pltpu.roll(f, z, 1)),
+            (in_x, pltpu.roll(f, lax.rem(z + LANES - EX + 1, LANES), 1)),
+        )
+        for k, (where, v) in enumerate(turned):
+            hsend[s, k] = jnp.where(where, v, hsend[s, k])
+
+    blank = jnp.zeros((B, LANES), F32)
+    for s in range(3):
         for k in range(4):
-            hsend[s, k] = jnp.zeros((B, LANES), F32)
-        lax.fori_loop(0, depth, loop, 0)
-
-    half_rows = B * depth // 2
-    chunk = half_rows // 8
-
-    def first_sums(i, carry):
+            hsend[s, k] = blank
+
+    def first_pass(z, carry):
         a, b, c = carry
-        lo = pl.ds(pl.multiple_of(i * chunk, 8), chunk)
-        hi = pl.ds(pl.multiple_of(half_rows + i * chunk, 8), chunk)
-        ur, ui, fr, fi = rit[lo, :], rit[hi, :], res[lo, :], res[hi, :]
-        return (
-            a + fold(ur * ur + ui * ui),
-            b + fold(ur * fr + ui * fi),
-            c + fold(ur * fi - ui * fr),
-        )
+        u, f = rlayer(rit, z), rlayer(res, z)
+        U[z] = u
+        R[z] = f
+        pack(0, z, f)
+        pack(1, z, u)
+        re_z, im_z = pair_terms(u, f)
+        return a + fold(u * u), b + re_z, c + im_z
 
     zero = jnp.zeros((8, LANES), F32)
     loads[0].wait()
     loads[1].wait()
-    sums = lax.fori_loop(0, 8, first_sums, (zero, zero, zero))
+    sums = lax.fori_loop(0, depth, first_pass, (zero, zero, zero))
     pl.semaphore_wait(barrier, G - 1 + X - 1)
     sum_start(0, *sums)
-
-    for s, ref, layers in ((0, res, R), (1, rit, U)):
-        for k, z in ((0, 0), (1, depth - 1)):
-            layers[z] = rlayer(ref, z)
-        halo_start(s, (0, 1))
-
-        def turned(z, ref=ref, layers=layers):
-            f = rlayer(ref, z)
-
-            @pl.when((z > 0) & (z < depth - 1))
-            def _():
-                layers[z] = f
-
-            return f
-
-        pack(s, turned)
-        if s == 0:
-            sum_middle(0)
-        halo_start(s, (2, 3, 4, 5))
+    for ks in ((2, 3), (0, 1), (4, 5)):
+        for s in range(2):
+            halo_start(s, ks)
+    sum_middle(0)
 
     for k in range(6):
         @pl.when(jnp.logical_not(faces[k][2]))
@@ -304,16 +280,15 @@
             z = 2 * j + q
             o = out[:, q * LANES:(q + 1) * LANES]
             I1[z] = o
+            pack(2, z, o)
             re_q, im_q = pair_terms(U[z], o)
             a, b, c = a + re_q, b + im_q, c + fold(o * o)
         return a, b, c
 
     sums = lax.fori_loop(0, depth // 2, apply_one, (zero, zero, zero))
     sum_start(1, *sums)
-    halo_start(2, (0, 1))
-    pack(2, lambda z: I1[z])
+    halo_start(2, (2, 3, 0, 1, 4, 5))
     sum_middle(1)
-    halo_start(2, (2, 3, 4, 5))
     re, im, square = sum_end(1)
     factor = jnp.sqrt(count / (square - (re * re + im * im) * inv))
     build(2, lambda z: I1[z], factor, re * inv, im * inv)

time: 43.2 us -> 42.1 us (0.975)
  Pallas kernels: 39.7 us -> 38.5 us
    pallas_call x1, Pallas kernels: 39.7 us -> 38.5 us  [local(): pl.pallas_call(functools.partial(kernel, G, X, B, depth), out_shape=(pltp...]
where the time goes in v4:
time: 42.1 us; the launch traced here: 41.9 us
  Pallas kernels  38.5 us (91%)
  between operations  1.93 us (5%)
  local copies, waits for them, and re-layouts  1.41 us (3%)
    pallas_call x1, Pallas kernels, local(): pl.pallas_call(functools.partial(kernel, G, X, B, depth), out_shape=(pltp...  38.5 us
    unnamed x2, local copies, waits for them, and re-layouts  1.41 us

profile of v4, /device:TPU:0, one launch (start us, length us, event | category | flops | bytes accessed | tf_op | source)
XLA Modules:
  0.0 41.9 jit_solution(6056722575721924983)
XLA Ops:
  1.9 38.5 %shard_map.122 = (f32[1152,128]{1,0:T(8,128)S(1)}, f32[8,128]{1,0:T(8,128)S(1)}) custom-call(f32[1152,128]{1,0:T(8,128)} %bitcast.17, f32[1152,128]{1,0:T(8,128)} %bitcast.18, f32[8,128]{1,0:T(8,128)} %bitcast.19, s32[8,128]{1,0:T(8,128)} %bitcast.20, s32[8,128]{1,0:T(8,128)} %bitcast.21, f32[144,144]{1,0:T(8,128)} %kb_in.1, f32[144,144]{1,0:T(8,128)} %kr_in.1, ...), custom_call_target="tpu_custom_call" | custom-call | tf_op jit(solution)/shard_map/pallas_call | solution.py:393
  40.5 0.8 %copy.17 = f32[144,8,1,128]{3,2,1,0:T(1,128)} copy(f32[144,8,1,128]{3,2,1,0:T(1,128)S(1)} %bitcast.15) | data formatting | bytes 1179648
  41.3 0.6 %copy.18 = f32[8,1,128]{2,1,0:T(1,128)} copy(f32[8,1,128]{2,1,0:T(1,128)S(1)} %bitcast.16) | data formatting | bytes 8192
